TPU v7x, 512 devices: a whole 4x8x8 slice. The times are simulated.
512 devices in a mesh: shot: 16 (over x_lo, z), tile: 32 (over y, x_hi, core).
Axes of the slice: x: 4 (x_hi: 2, x_lo: 2; x = x_hi * 2 + x_lo), y: 8, z: 8, core: 2. Of those that a mesh axis runs over, the one named last changes fastest.
Arguments:
- latent: bfloat16 [96, 16, 64, 64], P('tile', 'shot'), may hold values from -6 to 6
- kernel: bfloat16 [27, 64, 64], replicated, may hold values from -0.15625 to 0.15625
- conv_bias: float32 [64], replicated, may hold values from -3 to 3
- head_weight: bfloat16 [64], replicated, may hold values from -0.75 to 0.75
- density: float32 [192, 32, 128], P('tile'), may hold values from 1 to 2.5
- wave_prev: float32 [16, 192, 32, 128], P('shot', 'tile'), may hold values from -6 to 6
- wave_now: float32 [16, 192, 32, 128], P('shot', 'tile'), may hold values from -6 to 6
- adjoint_next: float32 [16, 192, 32, 128], P('shot', 'tile'), may hold values from -6 to 6
- adjoint_after: float32 [16, 192, 32, 128], P('shot', 'tile'), may hold values from -6 to 6
- source_cell: int32 [16], P('shot'), may hold values from 0 to 786431
- wavelet: float32 [16, 3], P('shot'), may hold values from -24 to 24
- receiver_cells: int32 [16, 128], P('shot'), may hold values from 0 to 786431
- observed: float32 [16, 3, 128], P('shot'), may hold values from -6 to 6
Outputs:
- latent_grad: float32 [96, 16, 64, 64], P('tile', 'shot')
- kernel_grad: float32 [27, 64, 64], replicated
- head_grad: float32 [64], replicated
- bias_grad: float32 [64], replicated
All inputs are finite; a program needn't handle non-finite values.
Results may differ from a plain program's by a relative error of at most 0.0034.
The roundings to bfloat16 on the way count: a program that leaves them out, or rounds other values in their place, can miss the bound.
Values may be sent and summed in bfloat16 or wider, within the bound.
No kernel may reach another device: no remote copies, remote signals or barrier semaphores. Data moves between devices by JAX's collectives and lax.ppermute only.
A program may use at most 64 MiB of HBM per device.

v0:
```python
import jax
import jax.numpy as jnp
from jax import lax
from jax.sharding import PartitionSpec as P

courant = 0.005
speed_low = 1.5
speed_span = 3.0


def padded_2(cells, sides, width):
    for axis, dim in sides:
        count = lax.axis_size(axis)
        ends = count - 1
        head = lax.slice_in_dim(cells, 0, width, axis=dim)
        tail = lax.slice_in_dim(cells, cells.shape[dim] - width, cells.shape[dim], axis=dim)
        cells = jnp.concatenate(
            [
                lax.ppermute(tail, axis, [(i, (i + 1) % count) for i in range(ends)]),
                cells,
                lax.ppermute(head, axis, [((i + 1) % count, i) for i in range(ends)]),
            ],
            axis=dim,
        )
    return cells


def upsample(coarse):
    coarse_x, coarse_z, channels, coarse_y = coarse.shape
    spread = jnp.broadcast_to(
        coarse[:, None, :, None, :, :, None], (coarse_x, 2, coarse_z, 2, channels, coarse_y, 2)
    )
    return spread.reshape(coarse_x * 2, coarse_z * 2, channels, coarse_y * 2)


def fold_children(fine):
    fine_x, fine_z, channels, fine_y = fine.shape
    grouped = fine.reshape(fine_x // 2, 2, fine_z // 2, 2, channels, fine_y // 2, 2)
    return jnp.sum(grouped, axis=(1, 3, 6))


def shifted_stack(padded, start_x, start_z, starts_y, cells_x, cells_z, cells_y):
    return jnp.concatenate(
        [
            padded[
                start_x : start_x + cells_x,
                start_z : start_z + cells_z,
                :,
                start_y : start_y + cells_y,
            ]
            for start_y in starts_y
        ],
        axis=2,
    )


def convolve(padded, kernel):
    cells_x = padded.shape[0] - 2
    cells_z = padded.shape[1] - 2
    channels = padded.shape[2]
    cells_y = padded.shape[3] - 2
    tap_table = kernel.reshape(3, 3, 3, channels, channels)
    result = jnp.zeros((cells_x, cells_z, channels, cells_y), jnp.float32)
    for offset_x in range(3):
        for offset_z in range(3):
            stacked = shifted_stack(
                padded, offset_x, offset_z, (0, 1, 2), cells_x, cells_z, cells_y
            )
            matrix = jnp.transpose(tap_table[offset_x, offset_z], (1, 0, 2)).reshape(
                channels, 3 * channels
            )
            result = result + jnp.einsum(
                "ok,abky->aboy", matrix, stacked, preferred_element_type=jnp.float32
            )
    return result


def kernel_terms(padded, grad_low):
    cells_x, cells_z, channels, cells_y = grad_low.shape
    pieces = []
    for offset_x in range(3):
        for offset_z in range(3):
            stacked = shifted_stack(
                padded, offset_x, offset_z, (0, 1, 2), cells_x, cells_z, cells_y
            )
            product = jnp.einsum(
                "aboy,abky->ok", grad_low, stacked, preferred_element_type=jnp.float32
            )
            pieces.append(jnp.transpose(product.reshape(channels, 3, channels), (1, 0, 2)))
    return jnp.stack(pieces).reshape(27, channels, channels)


def transposed(grad_padded, kernel):
    cells_x = grad_padded.shape[0] - 2
    cells_z = grad_padded.shape[1] - 2
    channels = grad_padded.shape[2]
    cells_y = grad_padded.shape[3] - 2
    tap_table = kernel.reshape(3, 3, 3, channels, channels)
    result = jnp.zeros((cells_x, cells_z, channels, cells_y), jnp.float32)
    for offset_x in range(3):
        for offset_z in range(3):
            stacked = shifted_stack(
                grad_padded, 2 - offset_x, 2 - offset_z, (2, 1, 0), cells_x, cells_z, cells_y
            )
            matrix = tap_table[offset_x, offset_z].reshape(3 * channels, channels)
            result = result + jnp.einsum(
                "kc,abky->abcy", matrix, stacked, preferred_element_type=jnp.float32
            )
    return result


def neighbours(padded):
    return (
        padded[2:, 1:-1, 1:-1],
        padded[:-2, 1:-1, 1:-1],
        padded[1:-1, 2:, 1:-1],
        padded[1:-1, :-2, 1:-1],
        padded[1:-1, 1:-1, 2:],
        padded[1:-1, 1:-1, :-2],
    )


def face_weights(padded_buoyancy):
    centre = padded_buoyancy[1:-1, 1:-1, 1:-1]
    return tuple((0.5 * (centre + beside) for beside in neighbours(padded_buoyancy)))


def apply_faces(padded, faces):
    centre = padded[1:-1, 1:-1, 1:-1]
    result = jnp.zeros_like(centre)
    for weight, beside in zip(faces, neighbours(padded)):
        result = result + weight * (beside - centre)
    return result


def propagate(
    laplace,
    coefficient,
    previous,
    current,
    following,
    beyond,
    anchor,
    source_cell,
    wavelet,
    receiver_cells,
    observed,
):
    field_shape = previous.shape
    field_cells = previous.size
    source_local = source_cell[0] - anchor
    source_owned = jnp.logical_and(source_local >= 0, source_local < field_cells).astype(
        jnp.float32
    )
    source_spot = jnp.clip(source_local, 0, field_cells - 1)
    receiver_local = receiver_cells[0] - anchor
    receiver_owned = jnp.logical_and(receiver_local >= 0, receiver_local < field_cells).astype(
        jnp.float32
    )
    receiver_spot = jnp.clip(receiver_local, 0, field_cells - 1)
    count_steps = wavelet.shape[1]
    laplacians = []
    residuals = []
    for instant in range(count_steps):
        laplacian = laplace(current)
        laplacians.append(laplacian)
        advanced = 2.0 * current - previous + coefficient * laplacian
        advanced = (
            advanced.reshape(-1)
            .at[source_spot]
            .add(source_owned * wavelet[0, instant])
            .reshape(field_shape)
        )
        residuals.append(
            receiver_owned * (advanced.reshape(-1)[receiver_spot] - observed[0, instant])
        )
        previous, current = (current, advanced)
    laplacians.append(laplace(current))
    coef_grad = following * laplacians[count_steps]
    for instant in reversed(range(count_steps)):
        preceding = 2.0 * following - beyond + laplace(coefficient * following)
        preceding = (
            preceding.reshape(-1).at[receiver_spot].add(residuals[instant]).reshape(field_shape)
        )
        coef_grad = coef_grad + preceding * laplacians[instant]
        beyond, following = (following, preceding)
    return coef_grad


def per_device(
    latent,
    kernel,
    conv_bias,
    head_weight,
    density,
    wave_prev,
    wave_now,
    adjoint_next,
    adjoint_after,
    source_cell,
    wavelet,
    receiver_cells,
    observed,
):
    extended = padded_2(upsample(latent), (("shot", 1), ("tile", 0)), 1)
    padded = jnp.pad(extended, ((0, 0), (0, 0), (0, 0), (1, 1)))
    pre_act = convolve(padded, kernel) + conv_bias[None, None, :, None]
    hidden = jax.nn.silu(pre_act).astype(jnp.bfloat16)
    logit = jnp.einsum("abcy,c->aby", hidden, head_weight, preferred_element_type=jnp.float32)
    squash = jax.nn.sigmoid(logit)
    velocity = speed_low + speed_span * squash
    tile_speed = lax.all_gather(velocity, "shot", axis=1, tiled=True)
    tile_cells = tile_speed.size
    buoyancy = 1.0 / density
    coefficient = courant * tile_speed * tile_speed * density
    factor = 2.0 * courant * tile_speed * density
    buoyancy_edges = padded_2(buoyancy, (("tile", 0),), 1)
    faces = face_weights(jnp.pad(buoyancy_edges, ((0, 0), (1, 1), (1, 1))))

    def laplace(field):
        field_edges = padded_2(field, (("tile", 0),), 1)
        return apply_faces(jnp.pad(field_edges, ((0, 0), (1, 1), (1, 1))), faces)

    anchor = lax.axis_index("tile") * tile_cells
    coef_grad = propagate(
        laplace,
        coefficient,
        wave_prev[0],
        wave_now[0],
        adjoint_next[0],
        adjoint_after[0],
        anchor,
        source_cell,
        wavelet,
        receiver_cells,
        observed,
    )
    strip_grad = lax.psum_scatter(coef_grad * factor, "shot", scatter_dimension=1, tiled=True)
    logit_grad = strip_grad * speed_span * squash * (1.0 - squash)
    head_part = jnp.einsum(
        "abcy,aby->c", hidden.astype(jnp.float32), logit_grad, precision=lax.Precision.HIGHEST
    )
    gate = jax.nn.sigmoid(pre_act)
    pre_grad = (
        logit_grad[:, :, None, :]
        * head_weight.astype(jnp.float32)[None, None, :, None]
        * (gate * (1.0 + pre_act * (1.0 - gate)))
    )
    bias_part = jnp.sum(pre_grad, axis=(0, 1, 3))
    grad_low = pre_grad.astype(jnp.bfloat16)
    kernel_part = kernel_terms(padded, grad_low)
    grad_edges = padded_2(grad_low, (("shot", 1), ("tile", 0)), 1)
    grad_padded = jnp.pad(grad_edges, ((0, 0), (0, 0), (0, 0), (1, 1)))
    latent_grad = fold_children(transposed(grad_padded, kernel))
    kernel_grad, head_grad, bias_grad = lax.psum(
        (kernel_part, head_part, bias_part), ("shot", "tile")
    )
    return (latent_grad, kernel_grad, head_grad, bias_grad)


def solution(mesh):
    return jax.shard_map(
        per_device,
        mesh=mesh,
        in_specs=(
            P("tile", "shot", None, None),
            P(),
            P(),
            P(),
            P("tile", None, None),
            P("shot", "tile", None, None),
            P("shot", "tile", None, None),
            P("shot", "tile", None, None),
            P("shot", "tile", None, None),
            P("shot"),
            P("shot", None),
            P("shot", None),
            P("shot", None, None),
        ),
        out_specs=(P("tile", "shot", None, None), P(), P(), P()),
        check_vma=False,
    )
```

profile of v0, /device:TPU:1, one launch (start us, length us, event | category | flops | bytes accessed | tf_op | source)
XLA Modules:
  0.0 589.9 jit_solution(18035886360403443610)
XLA Ops:
  7.2 0.9 copy.175
  8.4 4.8 collective-permute-start.1
  13.2 1.3 collective-permute-start.2
  14.5 0.7 slice_bitcast_fusion.6
  15.3 5.2 collective-permute-start.5
  20.5 2.2 collective-permute-start.7
  23.5 0.9 fusion.250
  26.8 2.4 collective-permute-start.3
  29.2 1.9 collective-permute-start.4
  31.4 5.0 collective-permute-done.4
  36.9 1.0 fusion.245
  42.4 32.4 %all_gather.3 = f32[6,32,128]{2,0,1:T(8,128)S(1)} all-gather(f32[6,2,128]{2,0,1:T(8,128)S(1)} %multiply_add_fusion.2), channel_id=1, replica_groups=mesh['shot'=16,'tile'=32] {'shot'}, dimensions={1}, use_global_device_ids=true | all-gather | bytes 104448 | tf_op jit(solution)/shard_map/all_gather | solution.py:212
  74.9 5.3 collective-permute-start
  80.3 6.1 %collective-permute-start.6 = (f32[1,32,128]{2,1,0:T(8,128)S(1)}, f32[1,32,128]{2,1,0:T(8,128)S(1)}, u32[]{:S(2)}, u32[]{:S(2)}) collective-permute-start(f32[1,32,128]{2,1,0:T(8,128)S(1)} %get-tuple-element.149), channel_id=1, source_target_pairs={{0,1},{1,2},{2,3},{3,4},{4,5},{5,6},{6,7},{7,8},{8,9},{9,10},{10,1... | collective-permute-start | bytes 49160 | tf_op jit(solution)/shard_map/ppermute | solution.py:19
  86.4 1.9 collective-permute-start.14
  88.4 5.1 collective-permute-start.15
  95.2 1.9 collective-permute-start.8
  97.1 5.7 collective-permute-start.9
  104.2 1.9 collective-permute-start.10
  106.1 5.7 collective-permute-start.11
  112.5 1.1 gather_fusion.2
  113.6 1.1 gather_fusion.1
  115.4 1.1 gather_fusion
  116.5 1.5 scatter_fusion
  118.1 1.9 collective-permute-start.16
  120.0 5.1 collective-permute-start.17
  125.2 1.9 collective-permute-start.12
  127.1 5.1 collective-permute-start.13
  132.6 1.5 scatter_fusion.1
  134.1 1.9 collective-permute-start.18
  136.0 5.5 collective-permute-start.19
  142.7 1.7 scatter_fusion.2
  144.4 0.9 fusion.136
  145.3 1.3 dynamic-slice.27
  147.3 136.4 %all-reduce.17.cloned.1.call-done = f32[6,32,128]{2,1,0:T(8,128)} async-done(((f32[6,32,128]{2,1,0:T(8,128)}), f32[6,32,128]{2,1,0:T(8,128)}) %all-reduce.17.cloned.1.call-update) | async-done | bytes 98320
  283.6 0.7 constant_dynamic-slice_fusion
  284.7 1.4 fusion.74
  292.0 1.7 collective-permute-start.20
  293.7 1.3 collective-permute-start.21
  295.7 1.2 copy.221
  297.0 2.1 collective-permute-done.21
  299.1 16.4 %collective-permute-start.22 = (bf16[1,4,64,128]{3,2,1,0:T(8,128)(2,1)S(1)}, bf16[1,4,64,128]{3,2,1,0:T(8,128)(2,1)S(1)}, u32[]{:S(2)}, u32[]{:S(2)}) collective-permute-start(bf16[1,4,64,128]{3,2,1,0:T(8,128)(2,1)S(1)} %get-tuple-element.129), channel_id=1, source_target_pairs={{0,1},{1,2},{2,3},{3,4},{4,5},{5,6},{6,7},{7,8},{8,9},{9,10},{10,1... | collective-permute-start | bytes 196616 | tf_op jit(solution)/shard_map/ppermute | solution.py:19
  315.5 1.9 collective-permute-start.23
  317.7 101.0 %all-reduce.11 = (f32[64]{0:T(128)}, f32[64]{0:T(128)}) all-reduce(f32[64]{0:T(128)S(1)} %convolution_bitcast_fusion, f32[64]{0:T(128)S(1)} %get-tuple-element.46), channel_id=1, replica_groups=mesh['shot'=16,'tile'=32] {'shot','tile'}, use_global_device_ids=true, to_apply=%region_7.8 | all-reduce | flops 128 | bytes 1024 | tf_op jit(solution)/shard_map/psum | solution.py:255
  419.5 1.0 fusion.244
  425.8 0.7 copy.222
  426.6 154.3 %all-reduce.15.cloned.1.call-done = f32[27,64,64]{2,1,0:T(8,128)} async-done(((f32[27,64,64]{2,1,0:T(8,128)}), f32[27,64,64]{2,1,0:T(8,128)}) %all-reduce.15.cloned.1.call-update) | async-done | bytes 442384 | tf_op jit(solution)/shard_map/psum | solution.py:255
  580.9 2.2 copy.315
  (240 shorter events, 24.4 us)
Async XLA Ops:
  7.2 16.3 %copy-start.3 = (bf16[27,64,64]{2,1,0:T(8,128)(2,1)S(1)}, bf16[27,64,64]{2,1,0:T(8,128)(2,1)}, u32[]{:S(2)}) copy-start(bf16[27,64,64]{2,1,0:T(8,128)(2,1)} %param.20) | copy-start | bytes 663556
  7.2 276.4 %all-reduce.17.cloned.1.call-start = ((), (), s32[]{:S(2)}) async-start(), calls=%async_computation.1 | async-start | bytes 196608
  8.4 18.3 %collective-permute-start.1 = (bf16[6,1,64,128]{3,2,1,0:T(8,128)(2,1)S(1)}, bf16[6,1,64,128]{3,2,1,0:T(8,128)(2,1)S(1)}, u32[]{:S(2)}, u32[]{:S(2)}) collective-permute-start(bf16[6,1,64,128]{3,2,1,0:T(8,128)(2,1)S(1)} %copy.176), channel_id=1, source_target_pairs={{0,32},{32,64},{64,96},{96,128},{128,160},{160,192},{192,224},{224... | collective-permute-start | bytes 294920 | tf_op jit(solution)/shard_map/ppermute | solution.py:19
  13.2 13.5 %collective-permute-start.2 = (bf16[6,1,64,128]{3,2,1,0:T(8,128)(2,1)S(1)}, bf16[6,1,64,128]{3,2,1,0:T(8,128)(2,1)S(1)}, u32[]{:S(2)}, u32[]{:S(2)}) collective-permute-start(bf16[6,1,64,128]{3,2,1,0:T(8,128)(2,1)S(1)} %copy.176), channel_id=1, source_target_pairs={{32,0},{64,32},{96,64},{128,96},{160,128},{192,160},{224,192},{256... | collective-permute-start | bytes 294920 | tf_op jit(solution)/shard_map/ppermute | solution.py:21
  15.3 15.9 %collective-permute-start.5 = (f32[1,32,128]{2,1,0:T(8,128)S(1)}, f32[1,32,128]{2,1,0:T(8,128)S(1)}, u32[]{:S(2)}, u32[]{:S(2)}) collective-permute-start(f32[1,32,128]{2,1,0:T(8,128)S(1)} %get-tuple-element.148), channel_id=1, source_target_pairs={{1,0},{2,1},{3,2},{4,3},{5,4},{6,5},{7,6},{8,7},{9,8},{10,9},{11,1... | collective-permute-start | bytes 49160 | tf_op jit(solution)/shard_map/ppermute | solution.py:21
  20.5 10.6 %collective-permute-start.7 = (f32[1,32,128]{2,1,0:T(8,128)S(1)}, f32[1,32,128]{2,1,0:T(8,128)S(1)}, u32[]{:S(2)}, u32[]{:S(2)}) collective-permute-start(f32[1,32,128]{2,1,0:T(8,128)S(1)} %get-tuple-element.147), channel_id=1, source_target_pairs={{0,1},{1,2},{2,3},{3,4},{4,5},{5,6},{6,7},{7,8},{8,9},{9,10},{10,1... | collective-permute-start | bytes 49160 | tf_op jit(solution)/shard_map/ppermute | solution.py:19
  23.5 1.9 copy-start.53
  24.4 6.7 %copy-start = (f32[1,6,32,128]{3,2,1,0:T(8,128)S(1)}, f32[1,6,32,128]{3,2,1,0:T(8,128)}, u32[]{:S(2)}) copy-start(f32[1,6,32,128]{3,2,1,0:T(8,128)} %param.25) | copy-start | bytes 294916
  26.8 4.5 collective-permute-start.3
  29.2 7.1 %collective-permute-start.4 = (bf16[1,4,64,128]{3,2,1,0:T(8,128)(2,1)S(1)}, bf16[1,4,64,128]{3,2,1,0:T(8,128)(2,1)S(1)}, u32[]{:S(2)}, u32[]{:S(2)}) collective-permute-start(bf16[1,4,64,128]{3,2,1,0:T(8,128)(2,1)S(1)} %get-tuple-element.134), channel_id=1, source_target_pairs={{1,0},{2,1},{3,2},{4,3},{5,4},{6,5},{7,6},{8,7},{9,8},{10,9},{11,1... | collective-permute-start | bytes 196616 | tf_op jit(solution)/shard_map/ppermute | solution.py:21
  38.0 2.1 copy-start.4
  38.0 2.1 copy-start.6
  38.0 2.7 copy-start.20
  38.0 2.7 copy-start.22
  38.0 3.0 copy-start.24
  38.0 3.0 copy-start.26
  38.0 3.3 copy-start.28
  38.0 3.3 copy-start.29
  38.4 2.3 copy-start.36
  38.4 2.6 copy-start.38
  38.4 2.9 copy-start.40
  41.6 33.2 %copy-start.1 = (f32[1,6,32,128]{3,2,1,0:T(8,128)S(1)}, f32[1,6,32,128]{3,2,1,0:T(8,128)}, u32[]{:S(2)}) copy-start(f32[1,6,32,128]{3,2,1,0:T(8,128)} %param.26) | copy-start | bytes 294916
  41.6 33.2 %copy-start.2 = (f32[6,32,128]{2,1,0:T(8,128)S(1)}, f32[6,32,128]{2,1,0:T(8,128)}, u32[]{:S(2)}) copy-start(f32[6,32,128]{2,1,0:T(8,128)} %param.23) | copy-start | bytes 294916
  42.0 52.4 %copy-start.41 = (bf16[6,2,64,128]{3,2,1,0:T(8,128)(2,1)}, bf16[6,2,64,128]{3,2,1,0:T(8,128)(2,1)S(1)}, u32[]{:S(2)}) copy-start(bf16[6,2,64,128]{3,2,1,0:T(8,128)(2,1)S(1)} %get-tuple-element.160) | copy-start | bytes 589828
  42.0 52.6 %copy-start.43 = (f32[1,6,32,128]{3,2,1,0:T(8,128)S(1)}, f32[1,6,32,128]{3,2,1,0:T(8,128)}, u32[]{:S(2)}) copy-start(f32[1,6,32,128]{3,2,1,0:T(8,128)} %param.27) | copy-start | bytes 294916
  74.9 18.6 %collective-permute-start = (f32[1,32,128]{2,1,0:T(8,128)S(1)}, f32[1,32,128]{2,1,0:T(8,128)S(1)}, u32[]{:S(2)}, u32[]{:S(2)}) collective-permute-start(f32[1,32,128]{2,1,0:T(8,128)S(1)} %get-tuple-element.150), channel_id=1, source_target_pairs={{1,0},{2,1},{3,2},{4,3},{5,4},{6,5},{7,6},{8,7},{9,8},{10,9},{11,1... | collective-permute-start | bytes 49160 | tf_op jit(solution)/shard_map/ppermute | solution.py:21
  80.3 13.3 %collective-permute-start.6 = (f32[1,32,128]{2,1,0:T(8,128)S(1)}, f32[1,32,128]{2,1,0:T(8,128)S(1)}, u32[]{:S(2)}, u32[]{:S(2)}) collective-permute-start(f32[1,32,128]{2,1,0:T(8,128)S(1)} %get-tuple-element.149), channel_id=1, source_target_pairs={{0,1},{1,2},{2,3},{3,4},{4,5},{5,6},{6,7},{7,8},{8,9},{9,10},{10,1... | collective-permute-start | bytes 49160 | tf_op jit(solution)/shard_map/ppermute | solution.py:19
  86.4 7.3 %collective-permute-start.14 = (f32[1,32,128]{2,1,0:T(8,128)S(1)}, f32[1,32,128]{2,1,0:T(8,128)S(1)}, u32[]{:S(2)}, u32[]{:S(2)}) collective-permute-start(f32[1,32,128]{2,1,0:T(8,128)S(1)} %get-tuple-element.153), channel_id=1, source_target_pairs={{1,0},{2,1},{3,2},{4,3},{5,4},{6,5},{7,6},{8,7},{9,8},{10,9},{11,1... | collective-permute-start | bytes 49160 | tf_op jit(solution)/shard_map/ppermute | solution.py:21
  88.4 6.0 %collective-permute-start.15 = (f32[1,32,128]{2,1,0:T(8,128)S(1)}, f32[1,32,128]{2,1,0:T(8,128)S(1)}, u32[]{:S(2)}, u32[]{:S(2)}) collective-permute-start(f32[1,32,128]{2,1,0:T(8,128)S(1)} %get-tuple-element.152), channel_id=1, source_target_pairs={{0,1},{1,2},{2,3},{3,4},{4,5},{5,6},{6,7},{7,8},{8,9},{9,10},{10,1... | collective-permute-start | bytes 49160 | tf_op jit(solution)/shard_map/ppermute | solution.py:19
  94.8 8.0 %copy-start.56 = (s32[1,128]{1,0:T(1,128)S(1)}, s32[1,128]{1,0:T(1,128)}, u32[]{:S(2)}) copy-start(s32[1,128]{1,0:T(1,128)} %param.30) | copy-start | bytes 1540
  95.2 8.3 %collective-permute-start.8 = (f32[1,32,128]{2,1,0:T(8,128)S(1)}, f32[1,32,128]{2,1,0:T(8,128)S(1)}, u32[]{:S(2)}, u32[]{:S(2)}) collective-permute-start(f32[1,32,128]{2,1,0:T(8,128)S(1)} %get-tuple-element.146), channel_id=1, source_target_pairs={{1,0},{2,1},{3,2},{4,3},{5,4},{6,5},{7,6},{8,7},{9,8},{10,9},{11,1... | collective-permute-start | bytes 49160 | tf_op jit(solution)/shard_map/ppermute | solution.py:21
  97.1 6.6 %collective-permute-start.9 = (f32[1,32,128]{2,1,0:T(8,128)S(1)}, f32[1,32,128]{2,1,0:T(8,128)S(1)}, u32[]{:S(2)}, u32[]{:S(2)}) collective-permute-start(f32[1,32,128]{2,1,0:T(8,128)S(1)} %get-tuple-element.145), channel_id=1, source_target_pairs={{0,1},{1,2},{2,3},{3,4},{4,5},{5,6},{6,7},{7,8},{8,9},{9,10},{10,1... | collective-permute-start | bytes 49160 | tf_op jit(solution)/shard_map/ppermute | solution.py:19
  104.2 10.6 %collective-permute-start.10 = (f32[1,32,128]{2,1,0:T(8,128)S(1)}, f32[1,32,128]{2,1,0:T(8,128)S(1)}, u32[]{:S(2)}, u32[]{:S(2)}) collective-permute-start(f32[1,32,128]{2,1,0:T(8,128)S(1)} %get-tuple-element.144), channel_id=1, source_target_pairs={{1,0},{2,1},{3,2},{4,3},{5,4},{6,5},{7,6},{8,7},{9,8},{10,9},{11,1... | collective-permute-start | bytes 49160 | tf_op jit(solution)/shard_map/ppermute | solution.py:21
  106.1 8.7 %collective-permute-start.11 = (f32[1,32,128]{2,1,0:T(8,128)S(1)}, f32[1,32,128]{2,1,0:T(8,128)S(1)}, u32[]{:S(2)}, u32[]{:S(2)}) collective-permute-start(f32[1,32,128]{2,1,0:T(8,128)S(1)} %get-tuple-element.143), channel_id=1, source_target_pairs={{0,1},{1,2},{2,3},{3,4},{4,5},{5,6},{6,7},{7,8},{8,9},{9,10},{10,1... | collective-permute-start | bytes 49160 | tf_op jit(solution)/shard_map/ppermute | solution.py:19
  118.1 14.2 %collective-permute-start.16 = (f32[1,32,128]{2,1,0:T(8,128)S(1)}, f32[1,32,128]{2,1,0:T(8,128)S(1)}, u32[]{:S(2)}, u32[]{:S(2)}) collective-permute-start(f32[1,32,128]{2,1,0:T(8,128)S(1)} %get-tuple-element.140), channel_id=1, source_target_pairs={{1,0},{2,1},{3,2},{4,3},{5,4},{6,5},{7,6},{8,7},{9,8},{10,9},{11,1... | collective-permute-start | bytes 49160 | tf_op jit(solution)/shard_map/ppermute | solution.py:21
  120.0 12.3 %collective-permute-start.17 = (f32[1,32,128]{2,1,0:T(8,128)S(1)}, f32[1,32,128]{2,1,0:T(8,128)S(1)}, u32[]{:S(2)}, u32[]{:S(2)}) collective-permute-start(f32[1,32,128]{2,1,0:T(8,128)S(1)} %get-tuple-element.139), channel_id=1, source_target_pairs={{0,1},{1,2},{2,3},{3,4},{4,5},{5,6},{6,7},{7,8},{8,9},{9,10},{10,1... | collective-permute-start | bytes 49160 | tf_op jit(solution)/shard_map/ppermute | solution.py:19
  125.2 16.4 %collective-permute-start.12 = (f32[1,32,128]{2,1,0:T(8,128)S(1)}, f32[1,32,128]{2,1,0:T(8,128)S(1)}, u32[]{:S(2)}, u32[]{:S(2)}) collective-permute-start(f32[1,32,128]{2,1,0:T(8,128)S(1)} %get-tuple-element.142), channel_id=1, source_target_pairs={{1,0},{2,1},{3,2},{4,3},{5,4},{6,5},{7,6},{8,7},{9,8},{10,9},{11,1... | collective-permute-start | bytes 49160 | tf_op jit(solution)/shard_map/ppermute | solution.py:21
  127.1 14.5 %collective-permute-start.13 = (f32[1,32,128]{2,1,0:T(8,128)S(1)}, f32[1,32,128]{2,1,0:T(8,128)S(1)}, u32[]{:S(2)}, u32[]{:S(2)}) collective-permute-start(f32[1,32,128]{2,1,0:T(8,128)S(1)} %get-tuple-element.141), channel_id=1, source_target_pairs={{0,1},{1,2},{2,3},{3,4},{4,5},{5,6},{6,7},{7,8},{8,9},{9,10},{10,1... | collective-permute-start | bytes 49160 | tf_op jit(solution)/shard_map/ppermute | solution.py:19
  134.1 7.6 %collective-permute-start.18 = (f32[1,32,128]{2,1,0:T(8,128)S(1)}, f32[1,32,128]{2,1,0:T(8,128)S(1)}, u32[]{:S(2)}, u32[]{:S(2)}) collective-permute-start(f32[1,32,128]{2,1,0:T(8,128)S(1)} %get-tuple-element.138), channel_id=1, source_target_pairs={{1,0},{2,1},{3,2},{4,3},{5,4},{6,5},{7,6},{8,7},{9,8},{10,9},{11,1... | collective-permute-start | bytes 49160 | tf_op jit(solution)/shard_map/ppermute | solution.py:21
  136.0 6.4 %collective-permute-start.19 = (f32[1,32,128]{2,1,0:T(8,128)S(1)}, f32[1,32,128]{2,1,0:T(8,128)S(1)}, u32[]{:S(2)}, u32[]{:S(2)}) collective-permute-start(f32[1,32,128]{2,1,0:T(8,128)S(1)} %get-tuple-element.137), channel_id=1, source_target_pairs={{0,1},{1,2},{2,3},{3,4},{4,5},{5,6},{6,7},{7,8},{8,9},{9,10},{10,1... | collective-permute-start | bytes 49160 | tf_op jit(solution)/shard_map/ppermute | solution.py:19
  145.3 435.6 %all-reduce.15.cloned.1.call-start = ((), (), s32[]{:S(2)}) async-start(), calls=%async_computation | async-start | bytes 1769472 | tf_op jit(solution)/shard_map/psum | solution.py:255
  284.4 1.7 copy-start.25
  284.4 1.7 copy-start.27
  292.0 5.0 collective-permute-start.20
  293.7 5.4 collective-permute-start.21
  296.9 20.5 %copy-start.42 = (bf16[6,2,64,128]{3,2,1,0:T(8,128)(2,1)S(1)}, bf16[6,2,64,128]{3,2,1,0:T(8,128)(2,1)}, u32[]{:S(2)}) copy-start(bf16[6,2,64,128]{3,2,1,0:T(8,128)(2,1)} %copy-done.41) | copy-start | bytes 589828
  299.1 119.6 %collective-permute-start.22 = (bf16[1,4,64,128]{3,2,1,0:T(8,128)(2,1)S(1)}, bf16[1,4,64,128]{3,2,1,0:T(8,128)(2,1)S(1)}, u32[]{:S(2)}, u32[]{:S(2)}) collective-permute-start(bf16[1,4,64,128]{3,2,1,0:T(8,128)(2,1)S(1)} %get-tuple-element.129), channel_id=1, source_target_pairs={{0,1},{1,2},{2,3},{3,4},{4,5},{5,6},{6,7},{7,8},{8,9},{9,10},{10,1... | collective-permute-start | bytes 196616 | tf_op jit(solution)/shard_map/ppermute | solution.py:19
  315.5 103.2 %collective-permute-start.23 = (bf16[1,4,64,128]{3,2,1,0:T(8,128)(2,1)S(1)}, bf16[1,4,64,128]{3,2,1,0:T(8,128)(2,1)S(1)}, u32[]{:S(2)}, u32[]{:S(2)}) collective-permute-start(bf16[1,4,64,128]{3,2,1,0:T(8,128)(2,1)S(1)} %get-tuple-element.130), channel_id=1, source_target_pairs={{1,0},{2,1},{3,2},{4,3},{5,4},{6,5},{7,6},{8,7},{9,8},{10,9},{11,1... | collective-permute-start | bytes 196616 | tf_op jit(solution)/shard_map/ppermute | solution.py:21
  (36 other events, 36.2 us)
Sparse Core Ops, SparseCore 0:
  145.4 138.1 all-reduce.16
  297.1 283.7 all-reduce.14
where the time goes:
time: 591 us; the launch traced here: 590 us
  waiting for transfers between devices  299 us (51%)
  blocking collectives  133 us (23%)
  starting transfers between devices  94.6 us (16%)
  local copies, waits for them, and re-layouts  24.3 us (4%)
  between operations  18.9 us (3%)
  other arithmetic  10.4 us (2%)
  matrix products  9.01 us (2%)
    psum x1, waiting for transfers between devices, per_device(): lax.psum((kernel_part, head_part, bias_part), ('shot', 'tile'))  154 us
    unnamed x3, waiting for transfers between devices  136 us
    psum x1, blocking collectives, per_device(): lax.psum((kernel_part, head_part, bias_part), ('shot', 'tile'))  101 us
    ppermute x12, starting transfers between devices, padded_2(): lax.ppermute(tail, axis, [(i, (i + 1) % count) for i in range(ends)])  66 us
    all_gather x1, blocking collectives, per_device(): tile_speed = lax.all_gather(velocity, 'shot', axis=1, tiled=True)  32.4 us
    ppermute x12, starting transfers between devices, padded_2(): lax.ppermute(head, axis, [((i + 1) % count, i) for i in range(ends)])  28.5 us
    unnamed x128, local copies, waits for them, and re-layouts  12.5 us
  transfers between devices with their start and end apart: 26, of which 7 were waited for; matrix products, arithmetic and copies ran while one was open for 3% of the time, Pallas kernels for 0%

commit v1 on v0

--- a/solution.py
+++ b/solution.py
@@ -253,7 +253,7 @@
     grad_padded = jnp.pad(grad_edges, ((0, 0), (0, 0), (0, 0), (1, 1)))
     latent_grad = fold_children(transposed(grad_padded, kernel))
     kernel_grad, head_grad, bias_grad = lax.psum(
-        (kernel_part, head_part, bias_part), ("shot", "tile")
+        lax.psum((kernel_part, head_part, bias_part), "tile"), "shot"
     )
     return (latent_grad, kernel_grad, head_grad, bias_grad)
 

time: 591 us -> 733 us (1.24); the launches traced: 590 us -> 721 us
  waiting for transfers between devices: 299 us -> 440 us
  blocking collectives: 133 us -> 125 us
    psum x1 -> x2, waiting for transfers between devices: 154 us -> 295 us  [the longest x1 161 us: per_device(): lax.psum((kernel_part, head_part, bias_part), 'tile')]
    psum x1 -> x2, blocking collectives: 101 us -> 92.2 us  [the longest x1 65.1 us: per_device(): lax.psum((kernel_part, head_part, bias_part), 'tile')]
    unnamed x3 -> x4, waiting for transfers between devices: 136 us -> 136 us
  transfers between devices with their start and end apart: 26 -> 27, of which waited for: 7 -> 8; matrix products, arithmetic and copies ran while one was open for 3% -> 2% of each run, Pallas kernels for 0% -> 0%
where the time goes in v1:
time: 733 us; the launch traced here: 721 us
  waiting for transfers between devices  440 us (60%)
  blocking collectives  125 us (17%)
  starting transfers between devices  94.6 us (13%)
  local copies, waits for them, and re-layouts  24.5 us (3%)
  between operations  18.7 us (3%)
  other arithmetic  10.4 us (1%)
  matrix products  9.01 us (1%)
    psum x1, waiting for transfers between devices, per_device(): lax.psum((kernel_part, head_part, bias_part), 'tile')  161 us
    unnamed x4, waiting for transfers between devices  136 us
    psum x1, waiting for transfers between devices, per_device(): lax.psum(lax.psum((kernel_part, head_part, bias_part), 'tile'), 'shot')  133 us
    ppermute x12, starting transfers between devices, padded_2(): lax.ppermute(tail, axis, [(i, (i + 1) % count) for i in range(ends)])  66 us
    psum x1, blocking collectives, per_device(): lax.psum((kernel_part, head_part, bias_part), 'tile')  65.1 us
    all_gather x1, blocking collectives, per_device(): tile_speed = lax.all_gather(velocity, 'shot', axis=1, tiled=True)  32.4 us
    ppermute x12, starting transfers between devices, padded_2(): lax.ppermute(head, axis, [((i + 1) % count, i) for i in range(ends)])  28.5 us
    psum x1, blocking collectives, per_device(): lax.psum(lax.psum((kernel_part, head_part, bias_part), 'tile'), 'shot')  27.1 us
  transfers between devices with their start and end apart: 27, of which 8 were waited for; matrix products, arithmetic and copies ran while one was open for 2% of the time, Pallas kernels for 0%

profile of v1, /device:TPU:1, one launch (start us, length us, event | category | flops | bytes accessed | tf_op | source)
XLA Modules:
  0.0 721.4 jit_solution(797878365370146137)
XLA Ops:
  7.2 0.9 copy.175
  8.4 4.8 collective-permute-start.1
  13.3 1.3 collective-permute-start.2
  15.3 5.2 collective-permute-start.5
  20.5 2.2 collective-permute-start.7
  23.5 0.9 fusion.250
  26.8 2.4 collective-permute-start.3
  29.2 1.9 collective-permute-start.4
  31.4 5.0 collective-permute-done.4
  36.9 1.0 fusion.245
  42.4 32.4 %all_gather.3 = f32[6,32,128]{2,0,1:T(8,128)S(1)} all-gather(f32[6,2,128]{2,0,1:T(8,128)S(1)} %multiply_add_fusion.2), channel_id=1, replica_groups=mesh['shot'=16,'tile'=32] {'shot'}, dimensions={1}, use_global_device_ids=true | all-gather | bytes 104448 | tf_op jit(solution)/shard_map/all_gather | solution.py:212
  74.9 5.3 collective-permute-start
  80.2 6.1 collective-permute-start.6
  86.4 1.9 collective-permute-start.14
  88.3 5.1 collective-permute-start.15
  95.1 1.9 collective-permute-start.8
  97.1 5.7 collective-permute-start.9
  104.2 1.9 collective-permute-start.10
  106.1 5.7 collective-permute-start.11
  112.5 1.1 gather_fusion.2
  113.6 1.1 gather_fusion.1
  115.3 1.1 gather_fusion
  116.5 1.5 scatter_fusion
  118.0 1.9 collective-permute-start.16
  120.0 5.1 collective-permute-start.17
  125.1 1.9 collective-permute-start.12
  127.0 5.1 collective-permute-start.13
  132.5 1.5 scatter_fusion.1
  134.1 1.9 collective-permute-start.18
  136.0 5.5 collective-permute-start.19
  142.7 1.7 scatter_fusion.2
  144.3 0.9 fusion.136
  145.3 1.3 dynamic-slice.27
  147.2 136.4 %all-reduce.21.cloned.1.call-done = f32[6,32,128]{2,1,0:T(8,128)} async-done(((f32[6,32,128]{2,1,0:T(8,128)}), f32[6,32,128]{2,1,0:T(8,128)}) %all-reduce.21.cloned.1.call-update) | async-done | bytes 98320
  283.6 0.7 constant_dynamic-slice_fusion
  284.7 1.4 fusion.74
  291.9 1.7 collective-permute-start.20
  293.7 1.3 collective-permute-start.21
  295.7 1.2 copy.221
  297.0 2.0 collective-permute-done.21
  299.0 16.4 %collective-permute-start.22 = (bf16[1,4,64,128]{3,2,1,0:T(8,128)(2,1)S(1)}, bf16[1,4,64,128]{3,2,1,0:T(8,128)(2,1)S(1)}, u32[]{:S(2)}, u32[]{:S(2)}) collective-permute-start(bf16[1,4,64,128]{3,2,1,0:T(8,128)(2,1)S(1)} %get-tuple-element.131), channel_id=1, source_target_pairs={{0,1},{1,2},{2,3},{3,4},{4,5},{5,6},{6,7},{7,8},{8,9},{9,10},{10,1... | collective-permute-start | bytes 196616 | tf_op jit(solution)/shard_map/ppermute | solution.py:19
  315.5 1.9 collective-permute-start.23
  317.6 65.1 %all-reduce.11 = (f32[64]{0:T(128)S(1)}, f32[64]{0:T(128)S(1)}) all-reduce(f32[64]{0:T(128)S(1)} %convolution_bitcast_fusion, f32[64]{0:T(128)S(1)} %get-tuple-element.48), channel_id=1, replica_groups=mesh['shot'=16,'tile'=32] {'tile'}, use_global_device_ids=true, to_apply=%region_8.9 | all-reduce | flops 128 | bytes 1024 | tf_op jit(solution)/shard_map/psum | solution.py:256
  382.7 27.1 %all-reduce.12 = (f32[64]{0:T(128)}, f32[64]{0:T(128)}) all-reduce(f32[64]{0:T(128)S(1)} %get-tuple-element.44, f32[64]{0:T(128)S(1)} %get-tuple-element.45), channel_id=1, replica_groups=mesh['shot'=16,'tile'=32] {'shot'}, use_global_device_ids=true, to_apply=%region_9.10 | all-reduce | flops 128 | bytes 1024 | tf_op jit(solution)/shard_map/psum | solution.py:255
  410.7 1.0 fusion.244
  415.4 161.3 %all-reduce.17.cloned.1.call-done = f32[27,64,64]{2,1,0:T(8,128)} async-done(((f32[27,64,64]{2,1,0:T(8,128)}), f32[27,64,64]{2,1,0:T(8,128)}) %all-reduce.17.cloned.1.call-update) | async-done | bytes 442384 | tf_op jit(solution)/shard_map/psum | solution.py:256
  579.3 133.3 %all-reduce.19.cloned.1.call-done = f32[27,64,64]{2,1,0:T(8,128)} async-done(((f32[27,64,64]{2,1,0:T(8,128)}), f32[27,64,64]{2,1,0:T(8,128)}) %all-reduce.19.cloned.1.call-update) | async-done | bytes 442384 | tf_op jit(solution)/shard_map/psum | solution.py:255
  712.7 2.2 copy.316
  (244 shorter events, 26.1 us)
Async XLA Ops:
  7.2 16.3 %copy-start.3 = (bf16[27,64,64]{2,1,0:T(8,128)(2,1)S(1)}, bf16[27,64,64]{2,1,0:T(8,128)(2,1)}, u32[]{:S(2)}) copy-start(bf16[27,64,64]{2,1,0:T(8,128)(2,1)} %param.20) | copy-start | bytes 663556
  7.2 276.4 %all-reduce.21.cloned.1.call-start = ((), (), s32[]{:S(2)}) async-start(), calls=%async_computation.2 | async-start | bytes 196608
  8.4 18.3 %collective-permute-start.1 = (bf16[6,1,64,128]{3,2,1,0:T(8,128)(2,1)S(1)}, bf16[6,1,64,128]{3,2,1,0:T(8,128)(2,1)S(1)}, u32[]{:S(2)}, u32[]{:S(2)}) collective-permute-start(bf16[6,1,64,128]{3,2,1,0:T(8,128)(2,1)S(1)} %copy.176), channel_id=1, source_target_pairs={{0,32},{32,64},{64,96},{96,128},{128,160},{160,192},{192,224},{224... | collective-permute-start | bytes 294920 | tf_op jit(solution)/shard_map/ppermute | solution.py:19
  13.3 13.5 %collective-permute-start.2 = (bf16[6,1,64,128]{3,2,1,0:T(8,128)(2,1)S(1)}, bf16[6,1,64,128]{3,2,1,0:T(8,128)(2,1)S(1)}, u32[]{:S(2)}, u32[]{:S(2)}) collective-permute-start(bf16[6,1,64,128]{3,2,1,0:T(8,128)(2,1)S(1)} %copy.176), channel_id=1, source_target_pairs={{32,0},{64,32},{96,64},{128,96},{160,128},{192,160},{224,192},{256... | collective-permute-start | bytes 294920 | tf_op jit(solution)/shard_map/ppermute | solution.py:21
  15.3 15.9 %collective-permute-start.5 = (f32[1,32,128]{2,1,0:T(8,128)S(1)}, f32[1,32,128]{2,1,0:T(8,128)S(1)}, u32[]{:S(2)}, u32[]{:S(2)}) collective-permute-start(f32[1,32,128]{2,1,0:T(8,128)S(1)} %get-tuple-element.150), channel_id=1, source_target_pairs={{1,0},{2,1},{3,2},{4,3},{5,4},{6,5},{7,6},{8,7},{9,8},{10,9},{11,1... | collective-permute-start | bytes 49160 | tf_op jit(solution)/shard_map/ppermute | solution.py:21
  20.5 10.6 %collective-permute-start.7 = (f32[1,32,128]{2,1,0:T(8,128)S(1)}, f32[1,32,128]{2,1,0:T(8,128)S(1)}, u32[]{:S(2)}, u32[]{:S(2)}) collective-permute-start(f32[1,32,128]{2,1,0:T(8,128)S(1)} %get-tuple-element.149), channel_id=1, source_target_pairs={{0,1},{1,2},{2,3},{3,4},{4,5},{5,6},{6,7},{7,8},{8,9},{9,10},{10,1... | collective-permute-start | bytes 49160 | tf_op jit(solution)/shard_map/ppermute | solution.py:19
  23.5 1.9 copy-start.53
  24.4 6.8 copy-start
  26.8 4.5 collective-permute-start.3
  29.2 7.1 collective-permute-start.4
  37.9 2.1 copy-start.4
  38.0 2.1 copy-start.6
  38.0 2.7 copy-start.20
  38.0 2.7 copy-start.22
  38.0 3.0 copy-start.24
  38.0 3.0 copy-start.26
  38.0 3.3 copy-start.28
  38.0 3.3 copy-start.29
  38.4 2.3 copy-start.36
  38.4 2.6 copy-start.38
  38.4 2.9 copy-start.40
  41.6 33.2 %copy-start.1 = (f32[1,6,32,128]{3,2,1,0:T(8,128)S(1)}, f32[1,6,32,128]{3,2,1,0:T(8,128)}, u32[]{:S(2)}) copy-start(f32[1,6,32,128]{3,2,1,0:T(8,128)} %param.26) | copy-start | bytes 294916
  41.6 33.2 %copy-start.2 = (f32[6,32,128]{2,1,0:T(8,128)S(1)}, f32[6,32,128]{2,1,0:T(8,128)}, u32[]{:S(2)}) copy-start(f32[6,32,128]{2,1,0:T(8,128)} %param.23) | copy-start | bytes 294916
  41.9 52.4 %copy-start.41 = (bf16[6,2,64,128]{3,2,1,0:T(8,128)(2,1)}, bf16[6,2,64,128]{3,2,1,0:T(8,128)(2,1)S(1)}, u32[]{:S(2)}) copy-start(bf16[6,2,64,128]{3,2,1,0:T(8,128)(2,1)S(1)} %get-tuple-element.162) | copy-start | bytes 589828
  41.9 52.6 %copy-start.43 = (f32[1,6,32,128]{3,2,1,0:T(8,128)S(1)}, f32[1,6,32,128]{3,2,1,0:T(8,128)}, u32[]{:S(2)}) copy-start(f32[1,6,32,128]{3,2,1,0:T(8,128)} %param.27) | copy-start | bytes 294916
  74.9 18.6 %collective-permute-start = (f32[1,32,128]{2,1,0:T(8,128)S(1)}, f32[1,32,128]{2,1,0:T(8,128)S(1)}, u32[]{:S(2)}, u32[]{:S(2)}) collective-permute-start(f32[1,32,128]{2,1,0:T(8,128)S(1)} %get-tuple-element.152), channel_id=1, source_target_pairs={{1,0},{2,1},{3,2},{4,3},{5,4},{6,5},{7,6},{8,7},{9,8},{10,9},{11,1... | collective-permute-start | bytes 49160 | tf_op jit(solution)/shard_map/ppermute | solution.py:21
  80.2 13.3 %collective-permute-start.6 = (f32[1,32,128]{2,1,0:T(8,128)S(1)}, f32[1,32,128]{2,1,0:T(8,128)S(1)}, u32[]{:S(2)}, u32[]{:S(2)}) collective-permute-start(f32[1,32,128]{2,1,0:T(8,128)S(1)} %get-tuple-element.151), channel_id=1, source_target_pairs={{0,1},{1,2},{2,3},{3,4},{4,5},{5,6},{6,7},{7,8},{8,9},{9,10},{10,1... | collective-permute-start | bytes 49160 | tf_op jit(solution)/shard_map/ppermute | solution.py:19
  86.4 7.3 %collective-permute-start.14 = (f32[1,32,128]{2,1,0:T(8,128)S(1)}, f32[1,32,128]{2,1,0:T(8,128)S(1)}, u32[]{:S(2)}, u32[]{:S(2)}) collective-permute-start(f32[1,32,128]{2,1,0:T(8,128)S(1)} %get-tuple-element.155), channel_id=1, source_target_pairs={{1,0},{2,1},{3,2},{4,3},{5,4},{6,5},{7,6},{8,7},{9,8},{10,9},{11,1... | collective-permute-start | bytes 49160 | tf_op jit(solution)/shard_map/ppermute | solution.py:21
  88.3 6.0 collective-permute-start.15
  94.8 8.0 %copy-start.56 = (s32[1,128]{1,0:T(1,128)S(1)}, s32[1,128]{1,0:T(1,128)}, u32[]{:S(2)}) copy-start(s32[1,128]{1,0:T(1,128)} %param.30) | copy-start | bytes 1540
  95.1 8.4 %collective-permute-start.8 = (f32[1,32,128]{2,1,0:T(8,128)S(1)}, f32[1,32,128]{2,1,0:T(8,128)S(1)}, u32[]{:S(2)}, u32[]{:S(2)}) collective-permute-start(f32[1,32,128]{2,1,0:T(8,128)S(1)} %get-tuple-element.148), channel_id=1, source_target_pairs={{1,0},{2,1},{3,2},{4,3},{5,4},{6,5},{7,6},{8,7},{9,8},{10,9},{11,1... | collective-permute-start | bytes 49160 | tf_op jit(solution)/shard_map/ppermute | solution.py:21
  97.1 6.6 collective-permute-start.9
  104.2 10.6 %collective-permute-start.10 = (f32[1,32,128]{2,1,0:T(8,128)S(1)}, f32[1,32,128]{2,1,0:T(8,128)S(1)}, u32[]{:S(2)}, u32[]{:S(2)}) collective-permute-start(f32[1,32,128]{2,1,0:T(8,128)S(1)} %get-tuple-element.146), channel_id=1, source_target_pairs={{1,0},{2,1},{3,2},{4,3},{5,4},{6,5},{7,6},{8,7},{9,8},{10,9},{11,1... | collective-permute-start | bytes 49160 | tf_op jit(solution)/shard_map/ppermute | solution.py:21
  106.1 8.7 %collective-permute-start.11 = (f32[1,32,128]{2,1,0:T(8,128)S(1)}, f32[1,32,128]{2,1,0:T(8,128)S(1)}, u32[]{:S(2)}, u32[]{:S(2)}) collective-permute-start(f32[1,32,128]{2,1,0:T(8,128)S(1)} %get-tuple-element.145), channel_id=1, source_target_pairs={{0,1},{1,2},{2,3},{3,4},{4,5},{5,6},{6,7},{7,8},{8,9},{9,10},{10,1... | collective-permute-start | bytes 49160 | tf_op jit(solution)/shard_map/ppermute | solution.py:19
  118.0 14.2 %collective-permute-start.16 = (f32[1,32,128]{2,1,0:T(8,128)S(1)}, f32[1,32,128]{2,1,0:T(8,128)S(1)}, u32[]{:S(2)}, u32[]{:S(2)}) collective-permute-start(f32[1,32,128]{2,1,0:T(8,128)S(1)} %get-tuple-element.142), channel_id=1, source_target_pairs={{1,0},{2,1},{3,2},{4,3},{5,4},{6,5},{7,6},{8,7},{9,8},{10,9},{11,1... | collective-permute-start | bytes 49160 | tf_op jit(solution)/shard_map/ppermute | solution.py:21
  120.0 12.3 %collective-permute-start.17 = (f32[1,32,128]{2,1,0:T(8,128)S(1)}, f32[1,32,128]{2,1,0:T(8,128)S(1)}, u32[]{:S(2)}, u32[]{:S(2)}) collective-permute-start(f32[1,32,128]{2,1,0:T(8,128)S(1)} %get-tuple-element.141), channel_id=1, source_target_pairs={{0,1},{1,2},{2,3},{3,4},{4,5},{5,6},{6,7},{7,8},{8,9},{9,10},{10,1... | collective-permute-start | bytes 49160 | tf_op jit(solution)/shard_map/ppermute | solution.py:19
  125.1 16.4 %collective-permute-start.12 = (f32[1,32,128]{2,1,0:T(8,128)S(1)}, f32[1,32,128]{2,1,0:T(8,128)S(1)}, u32[]{:S(2)}, u32[]{:S(2)}) collective-permute-start(f32[1,32,128]{2,1,0:T(8,128)S(1)} %get-tuple-element.144), channel_id=1, source_target_pairs={{1,0},{2,1},{3,2},{4,3},{5,4},{6,5},{7,6},{8,7},{9,8},{10,9},{11,1... | collective-permute-start | bytes 49160 | tf_op jit(solution)/shard_map/ppermute | solution.py:21
  127.0 14.5 %collective-permute-start.13 = (f32[1,32,128]{2,1,0:T(8,128)S(1)}, f32[1,32,128]{2,1,0:T(8,128)S(1)}, u32[]{:S(2)}, u32[]{:S(2)}) collective-permute-start(f32[1,32,128]{2,1,0:T(8,128)S(1)} %get-tuple-element.143), channel_id=1, source_target_pairs={{0,1},{1,2},{2,3},{3,4},{4,5},{5,6},{6,7},{7,8},{8,9},{9,10},{10,1... | collective-permute-start | bytes 49160 | tf_op jit(solution)/shard_map/ppermute | solution.py:19
  134.1 7.6 %collective-permute-start.18 = (f32[1,32,128]{2,1,0:T(8,128)S(1)}, f32[1,32,128]{2,1,0:T(8,128)S(1)}, u32[]{:S(2)}, u32[]{:S(2)}) collective-permute-start(f32[1,32,128]{2,1,0:T(8,128)S(1)} %get-tuple-element.140), channel_id=1, source_target_pairs={{1,0},{2,1},{3,2},{4,3},{5,4},{6,5},{7,6},{8,7},{9,8},{10,9},{11,1... | collective-permute-start | bytes 49160 | tf_op jit(solution)/shard_map/ppermute | solution.py:21
  136.0 6.4 collective-permute-start.19
  145.2 431.5 %all-reduce.17.cloned.1.call-start = ((), (), s32[]{:S(2)}) async-start(), calls=%async_computation | async-start | bytes 1769472 | tf_op jit(solution)/shard_map/psum | solution.py:256
  291.9 5.0 collective-permute-start.20
  293.7 5.4 collective-permute-start.21
  296.9 20.5 %copy-start.42 = (bf16[6,2,64,128]{3,2,1,0:T(8,128)(2,1)S(1)}, bf16[6,2,64,128]{3,2,1,0:T(8,128)(2,1)}, u32[]{:S(2)}) copy-start(bf16[6,2,64,128]{3,2,1,0:T(8,128)(2,1)} %copy-done.41) | copy-start | bytes 589828
  296.9 415.7 %all-reduce.19.cloned.1.call-start = ((), (), s32[]{:S(2)}) async-start(), calls=%async_computation.1 | async-start | bytes 1769472 | tf_op jit(solution)/shard_map/psum | solution.py:255
  299.0 110.8 %collective-permute-start.22 = (bf16[1,4,64,128]{3,2,1,0:T(8,128)(2,1)S(1)}, bf16[1,4,64,128]{3,2,1,0:T(8,128)(2,1)S(1)}, u32[]{:S(2)}, u32[]{:S(2)}) collective-permute-start(bf16[1,4,64,128]{3,2,1,0:T(8,128)(2,1)S(1)} %get-tuple-element.131), channel_id=1, source_target_pairs={{0,1},{1,2},{2,3},{3,4},{4,5},{5,6},{6,7},{7,8},{8,9},{9,10},{10,1... | collective-permute-start | bytes 196616 | tf_op jit(solution)/shard_map/ppermute | solution.py:19
  315.5 94.4 %collective-permute-start.23 = (bf16[1,4,64,128]{3,2,1,0:T(8,128)(2,1)S(1)}, bf16[1,4,64,128]{3,2,1,0:T(8,128)(2,1)S(1)}, u32[]{:S(2)}, u32[]{:S(2)}) collective-permute-start(bf16[1,4,64,128]{3,2,1,0:T(8,128)(2,1)S(1)} %get-tuple-element.132), channel_id=1, source_target_pairs={{1,0},{2,1},{3,2},{4,3},{5,4},{6,5},{7,6},{8,7},{9,8},{10,9},{11,1... | collective-permute-start | bytes 196616 | tf_op jit(solution)/shard_map/ppermute | solution.py:21
  415.1 161.7 %copy-start.46 = (bf16[1,1,3,64,64]{4,3,2,1,0:T(8,128)(2,1)S(1)}, bf16[1,1,3,64,64]{4,3,2,1,0:T(8,128)(2,1)}, u32[]{:S(2)}) copy-start(bf16[1,1,3,64,64]{4,3,2,1,0:T(8,128)(2,1)} %get-tuple-element.122) | copy-start | bytes 73732
  (37 other events, 38.9 us)
Sparse Core Ops, SparseCore 0:
  145.3 138.1 all-reduce.20
  297.1 279.6 all-reduce.16
  579.7 132.9 all-reduce.18
